TPU v7x, 32 devices: a whole 2x2x4 slice. The times are simulated.
32 devices in a mesh: dp: 8 (over y, x, core), feat: 4 (over z).
Axes of the slice: x: 2, y: 2, z: 4, core: 2. Of those that a mesh axis runs over, the one named last changes fastest.
Arguments:
- images: bfloat16 [2048, 3072], P(('dp', 'feat')), may hold values from -6 to 6
- labels: int32 [2048], P('dp'), may hold values from 0 to 999
- predictions: float32 [2048, 1000], P('dp'), may hold values from -2 to 2
- filters: bfloat16 [75, 512], P(None, 'feat'), may hold values from -0.75 to 0.75
- biases: float32 [512], P('feat'), may hold values from -3 to 3
Outputs:
- weights: float32 [2048, 1000], P('feat')
- new_residual: float32 [2048, 1000], P(('dp', 'feat'))
All inputs are finite; a program needn't handle non-finite values.
Results may differ from a plain program's by a relative error of at most 0.007.
The roundings to bfloat16 on the way count: a program that leaves them out, or rounds other values in their place, can miss the bound.
Values may be sent and summed in bfloat16 or wider, within the bound.
A program may use at most 192 MiB of HBM per device.

v0:
```python
import math

import jax
import jax.numpy as jnp
from jax import lax
from jax.sharding import PartitionSpec as P

SIDE = 32
CHAN = 3
KSIZE = 5


def chol_solve(factor, rhs):
    middle = lax.linalg.triangular_solve(factor, rhs, left_side=True, lower=True, transpose_a=False)
    return lax.linalg.triangular_solve(factor, middle, left_side=True, lower=True, transpose_a=True)


def split_parts(values):
    upper = values.astype(jnp.bfloat16)
    lower = (values - upper.astype(jnp.float32)).astype(jnp.bfloat16)
    return (upper, lower)


def left_product(feats, other):
    return lax.dot_general(
        feats, other, (((0,), (0,)), ((), ())), preferred_element_type=jnp.float32
    )


def conv_pool(imgs, kernel, offsets):
    count = imgs.shape[0]
    filt_count = kernel.shape[3]
    pics = imgs.reshape(count, SIDE, SIDE, CHAN)
    response = lax.conv_general_dilated(
        pics,
        kernel,
        (1, 1),
        "VALID",
        dimension_numbers=("NHWC", "HWIO", "NHWC"),
        preferred_element_type=jnp.float32,
    )
    response = jnp.maximum(response + offsets, 0.0)
    half = (SIDE - KSIZE + 1) // 2
    pooled = response.reshape(count, 2, half, 2, half, filt_count).mean(axis=(2, 4))
    return jnp.transpose(pooled, (0, 3, 1, 2)).reshape(count, 4 * filt_count).astype(jnp.bfloat16)


def shards(images, labels, predictions, filters, biases):
    filt_count = filters.shape[1]
    kernel = filters.reshape(KSIZE, KSIZE, CHAN, filt_count)
    share = images.shape[0]
    total_images = share * lax.axis_size("feat") * lax.axis_size("dp")
    piece = lax.all_gather(images, "feat", axis=0, tiled=True)
    count = piece.shape[0]
    group = math.gcd(count, 128)
    blocks = piece.reshape(count // group, group, piece.shape[1])
    out = lax.map(lambda part: conv_pool(part, kernel, biases), blocks)
    feats = out.reshape(count, 4 * filt_count)
    width = feats.shape[1]
    residual = (
        labels[:, None] == jnp.arange(predictions.shape[1], dtype=jnp.int32)[None, :]
    ).astype(jnp.float32) - predictions
    res_upper, res_lower = split_parts(residual)
    gram = left_product(feats, feats)
    cross = left_product(feats, res_upper) + left_product(feats, res_lower)
    gram, cross = lax.psum((gram, cross), "dp")
    gram = gram / total_images + 0.5 * jnp.eye(width, dtype=jnp.float32)
    cross = cross / total_images
    factor = jnp.linalg.cholesky(gram)
    solved = chol_solve(factor, cross)
    sol_upper, sol_lower = split_parts(solved)
    fitted = lax.psum_scatter(
        (
            jnp.dot(feats, sol_upper, preferred_element_type=jnp.float32)
            + jnp.dot(feats, sol_lower, preferred_element_type=jnp.float32)
        ).astype(jnp.bfloat16),
        "feat",
        scatter_dimension=0,
        tiled=True,
    ).astype(jnp.float32)
    mine = lax.dynamic_slice_in_dim(residual, lax.axis_index("feat") * share, share, 0)
    return (solved, mine - fitted)


def solution(mesh):
    placed = (P(("dp", "feat"), None), P("dp"), P("dp", None), P(None, "feat"), P("feat"))
    return jax.shard_map(
        shards,
        mesh=mesh,
        in_specs=placed,
        out_specs=(P("feat", None), P(("dp", "feat"), None)),
        check_vma=False,
    )
```

profile of v0, /device:TPU:0, one launch (start us, length us, event | category | flops | bytes accessed | tf_op | source)
XLA Modules:
  0.0 392.2 jit_solution(4086881810303995427)
XLA Ops:
  8.7 1.6 copy.24
  10.3 1.1 convert_subtract_fusion
  11.4 38.0 %all-gather.2.cloned.1.call-done = bf16[256,3072]{1,0:T(8,128)(2,1)} async-done(((bf16[64,3072]{1,0:T(8,128)(2,1)}), bf16[256,3072]{1,0:T(8,128)(2,1)}) %all-gather.2.cloned.1.call-update) | async-done | bytes 1572880 | tf_op jit(solution)/shard_map/all_gather | solution.py:53
  49.4 76.4 %while.11 = (s32[]{:T(128)}, bf16[2,128,512]{1,2,0:T(8,128)(2,1)}, bf16[2,128,3072]{2,1,0:T(8,128)(2,1)}, bf16[5,5,3,128]{3,2,1,0:T(4,128)(2,1)S(1)}, f32[128]{0:T(128)S(1)}, /*index=5*/s32[]{:T(128)}, f32[]{:T(128)}) while((s32[]{:T(128)}, bf16[2,128,512]{1,2,0:T(8,128)(2,1)}, bf16[2,128,3072]{2,1,0:T(8,128)(2,1)}, ...), condition=%wide.region_2.3_spmd, body=%wide.region_0.2_spmd.sunk | while | flops 1965359104 | bytes 111562120 | solution.py:57
  49.4 1.2 constant_dynamic-slice_fusion.4
  51.4 19.1 %add_maximum_fusion.2 = f32[128,28,28,128]{3,0,2,1:T(8,128)} fusion(f32[128]{0:T(128)S(1)} %get-tuple-element.167, bf16[128,32,32,3]{0,3,2,1:T(4,128)(2,1)S(1)} %reshape.101, bf16[5,5,3,128]{3,2,1,0:T(4,128)(2,1)S(1)} %get-tuple-element.166), kind=kOutput, calls=%fused_computation.clone.1 | convolution fusion | flops 1952448512 | bytes 52186368 | tf_op jit(solution)/shard_map/while/body/eval_jaxpr/conv_general_dilated | solution.py:34
  70.5 16.2 %reduce_sum.10 = f32[128,2,2,128]{3,0,2,1:T(8,128)S(1)} reduce(f32[128,2,14,2,14,128]{5,0,4,3,2,1:T(8,128)} %bitcast.85, f32[]{:T(128)} %constant.173.clone.1..sunk), dimensions={2,4}, to_apply=%region_1.1 | reduce | flops 12779520 | bytes 51642372 | tf_op jit(solution)/shard_map/while/body/eval_jaxpr/reduce_sum | solution.py:44
  87.6 1.2 constant_dynamic-slice_fusion.4
  89.6 19.1 %add_maximum_fusion.2 = f32[128,28,28,128]{3,0,2,1:T(8,128)} fusion(f32[128]{0:T(128)S(1)} %get-tuple-element.167, bf16[128,32,32,3]{0,3,2,1:T(4,128)(2,1)S(1)} %reshape.101, bf16[5,5,3,128]{3,2,1,0:T(4,128)(2,1)S(1)} %get-tuple-element.166), kind=kOutput, calls=%fused_computation.clone.1 | convolution fusion | flops 1952448512 | bytes 52186368 | tf_op jit(solution)/shard_map/while/body/eval_jaxpr/conv_general_dilated | solution.py:34
  108.7 16.2 %reduce_sum.10 = f32[128,2,2,128]{3,0,2,1:T(8,128)S(1)} reduce(f32[128,2,14,2,14,128]{5,0,4,3,2,1:T(8,128)} %bitcast.85, f32[]{:T(128)} %constant.173.clone.1..sunk), dimensions={2,4}, to_apply=%region_1.1 | reduce | flops 12779520 | bytes 51642372 | tf_op jit(solution)/shard_map/while/body/eval_jaxpr/reduce_sum | solution.py:44
  125.8 1.2 copy.23
  126.9 2.4 convolution_bitcast_fusion
  129.8 1.8 convolution_add_fusion
  131.9 68.3 %all-reduce.4.cloned.1.call-done = (f32[512,1000]{0,1:T(8,128)}, f32[512,512]{1,0:T(8,128)}) async-done(((f32[512,1000]{0,1:T(8,128)}, f32[512,512]{1,0:T(8,128)}), (f32[512,1000]{0,1:T(8,128)}, f32[512,512]{1,0:T(8,128)})) %all-reduce.4.cloned.1.call-update) | async-done | bytes 3096592 | tf_op jit(solution)/shard_map/psum | solution.py:66
  200.1 2.4 select_add_fusion
  202.6 1.6 copy.22
  204.4 1.0 copy-done.3
  205.4 11.7 %cholesky.103 = f32[128,128]{1,0:T(8,128)S(1)} custom-call(f32[128,128]{1,0:T(8,128)S(1)} %cholesky.263), custom_call_target="Cholesky" | custom-call | tf_op jit(solution)/shard_map/jit(cholesky)/cholesky | solution.py:69
  217.2 9.8 %custom-call.32 = f32[1,128,128]{1,2,0:T(8,128)S(1)} custom-call(f32[1,128,128]{2,1,0:T(8,128)S(1)} %get-tuple-element.84), custom_call_target="InvertDiagBlocksLowerTriangular" | custom-call | tf_op jit(solution)/shard_map/jit(cholesky)/cholesky | solution.py:69
  227.0 1.2 constant_dynamic-update-slice_fusion.4
  228.3 1.3 convolution_subtract_fusion.4
  229.6 11.7 %cholesky.215 = f32[128,128]{1,0:T(8,128)S(1)} custom-call(f32[128,128]{1,0:T(8,128)S(1)} %cholesky.267), custom_call_target="Cholesky" | custom-call | tf_op jit(solution)/shard_map/jit(cholesky)/cholesky | solution.py:69
  241.3 10.2 %custom-call.33 = f32[1,128,128]{1,2,0:T(8,128)S(1)} custom-call(f32[1,128,128]{2,1,0:T(8,128)S(1)} %get-tuple-element.81), custom_call_target="InvertDiagBlocksLowerTriangular" | custom-call | tf_op jit(solution)/shard_map/jit(cholesky)/cholesky | solution.py:69
  251.8 1.3 convolution_subtract_fusion.5
  253.1 11.7 %cholesky.236 = f32[128,128]{1,0:T(8,128)S(1)} custom-call(f32[128,128]{1,0:T(8,128)S(1)} %cholesky.272), custom_call_target="Cholesky" | custom-call | tf_op jit(solution)/shard_map/jit(cholesky)/cholesky | solution.py:69
  265.5 9.8 %custom-call.34 = f32[1,128,128]{1,2,0:T(8,128)S(1)} custom-call(f32[1,128,128]{2,1,0:T(8,128)S(1)} %get-tuple-element.78), custom_call_target="InvertDiagBlocksLowerTriangular" | custom-call | tf_op jit(solution)/shard_map/jit(cholesky)/cholesky | solution.py:69
  275.5 1.2 convolution_subtract_fusion.6
  276.7 11.7 %cholesky.253 = f32[128,128]{1,0:T(8,128)S(1)} custom-call(f32[128,128]{1,0:T(8,128)S(1)} %convolution_subtract_fusion.6), custom_call_target="Cholesky" | custom-call | tf_op jit(solution)/shard_map/jit(cholesky)/cholesky | solution.py:69
  292.6 10.1 %while.12 = (s32[]{:T(128)}, f32[512,512]{1,0:T(8,128)S(1)}, s32[4,2]{0,1:T(2,128)S(1)}, f32[4,128,128]{2,1,0:T(8,128)}, s32[]{:T(128)}) while((s32[]{:T(128)}, f32[512,512]{1,0:T(8,128)S(1)}, s32[4,2]{0,1:T(2,128)S(1)}, f32[4,128,128]{2,1,0:T(8,128)}, s32[]{:T(128)}) %tuple.50), condition=%wide.while_cond, body=%wide.while_body.sunk | while | flops 2 | bytes 132705 | solution.py:15
  293.2 1.9 bitcast_dynamic-update-slice_fusion.2
  295.7 1.9 bitcast_dynamic-update-slice_fusion.2
  298.2 1.9 bitcast_dynamic-update-slice_fusion.2
  300.7 1.9 bitcast_dynamic-update-slice_fusion.2
  302.6 40.1 %custom-call.35 = f32[4,128,128]{1,2,0:T(8,128)S(1)} custom-call(f32[4,128,128]{2,1,0:T(8,128)} %get-tuple-element.37), custom_call_target="InvertDiagBlocksLowerTriangular" | custom-call | tf_op jit(solution)/shard_map/triangular_solve | solution.py:15
  342.8 1.8 broadcast_multiply_fusion
  345.5 1.0 convolution_subtract_fusion.3
  347.5 1.0 convolution_subtract_fusion.1
  349.4 1.8 fusion.17
  352.1 1.0 fusion.57
  353.1 1.0 convolution_subtract_fusion.2
  354.1 1.0 fusion.55
  355.1 1.0 convolution_subtract_fusion
  356.1 1.2 fusion.53
  357.3 1.8 fusion.14
  359.1 1.0 fusion.52
  360.7 1.3 fusion.13
  362.0 21.8 %reduce-scatter.2.cloned.1.call-done = bf16[64,1000]{1,0:T(8,128)(2,1)} async-done(((bf16[256,1000]{1,0:T(8,128)(2,1)}), bf16[64,1000]{1,0:T(8,128)(2,1)}) %reduce-scatter.2.cloned.1.call-update) | async-done | bytes 128016 | tf_op jit(solution)/shard_map/reduce_scatter | solution.py:72
  383.8 1.6 convert_subtract_fusion.1
  (70 shorter events, 15.6 us)
Async XLA Ops:
  7.2 3.1 copy-start.6
  7.2 42.2 %all-gather.2.cloned.1.call-start = ((), (), s32[]{:S(2)}) async-start(), calls=%async_computation.1 | async-start | bytes 1966080 | tf_op jit(solution)/shard_map/all_gather | solution.py:53
  7.9 192.2 %all-reduce.4.cloned.1.call-start = ((), (), s32[]{:S(2)}) async-start(), calls=%async_computation.3 | async-start | bytes 6193152 | tf_op jit(solution)/shard_map/psum | solution.py:66
  8.7 40.7 %copy-start.7 = (f32[128]{0:T(128)S(1)}, f32[128]{0:T(128)}, u32[]{:S(2)}) copy-start(f32[128]{0:T(128)} %param.11) | copy-start | bytes 1540
  70.5 16.3 %copy-start.4 = (bf16[2,128,512]{1,2,0:T(8,128)(2,1)S(1)}, bf16[2,128,512]{1,2,0:T(8,128)(2,1)}, u32[]{:S(2)}) copy-start(bf16[2,128,512]{1,2,0:T(8,128)(2,1)} %get-tuple-element.157) | copy-start | bytes 786436 | tf_op jit(solution)/shard_map/while
  86.9 0.7 copy-start.5
  108.7 16.3 %copy-start.4 = (bf16[2,128,512]{1,2,0:T(8,128)(2,1)S(1)}, bf16[2,128,512]{1,2,0:T(8,128)(2,1)}, u32[]{:S(2)}) copy-start(bf16[2,128,512]{1,2,0:T(8,128)(2,1)} %get-tuple-element.157) | copy-start | bytes 786436 | tf_op jit(solution)/shard_map/while
  125.1 0.7 copy-start.5
  125.8 3.6 copy-start.1
  131.6 252.2 %reduce-scatter.2.cloned.1.call-start = ((), (), s32[]{:S(2)}) async-start(), calls=%async_computation.2 | async-start | bytes 655360 | tf_op jit(solution)/shard_map/reduce_scatter | solution.py:72
  200.1 4.0 %copy-start.2 = (f32[512,512]{1,0:T(8,128)S(1)}, f32[512,512]{1,0:T(8,128)}, u32[]{:S(2)}) copy-start(f32[512,512]{1,0:T(8,128)} %get-tuple-element.72) | copy-start | bytes 3145732
  204.4 1.0 copy-start.3
  360.2 1.8 copy-start
Sparse Core Ops, SparseCore 0:
  9.6 39.7 all-gather.1
  131.7 68.3 all-reduce.3
  362.1 21.6 reduce-scatter.1
where the time goes:
time: 397 us; the launch traced here: 392 us
  other arithmetic  159 us (40%)
  waiting for transfers between devices  129 us (32%)
  matrix products  65.5 us (16%)
  local copies, waits for them, and re-layouts  21.8 us (5%)
  between operations  16.8 us (4%)
    another operation x14, other arithmetic, shards(): factor = jnp.linalg.cholesky(gram)  78.9 us
    psum x1, waiting for transfers between devices, shards(): gram, cross = lax.psum((gram, cross), 'dp')  68.3 us
    another operation x4, other arithmetic, chol_solve(): lax.linalg.triangular_solve(factor, middle, left_side=True, lower=True, t...  40.4 us
    conv_general_dilated x2, matrix products, conv_pool(): lax.conv_general_dilated(pics, kernel, (1, 1), 'VALID', dimension_numbers...  38.2 us
    all_gather x1, waiting for transfers between devices, shards(): piece = lax.all_gather(images, 'feat', axis=0, tiled=True)  38 us
    reduce_sum x2, other arithmetic, conv_pool(): response.reshape(count, 2, half, 2, half, filt_count).mean(axis=(2, 4))  32.3 us
    reduce_scatter x1, waiting for transfers between devices, shards(): lax.psum_scatter((jnp.dot(feats, sol_upper, preferred_element_type=jnp.fl...  21.8 us
    another operation x12, local copies, waits for them, and re-layouts  10 us
  transfers between devices with their start and end apart: 3, of which 3 were waited for; matrix products, arithmetic and copies ran while one was open for 1% of the time, Pallas kernels for 0%

commit v1 on v0

v1 whole, which is shorter than its diff:
```python
import functools

import jax
import jax.numpy as jnp
import ml_dtypes
import numpy as np
from jax import lax
from jax.experimental import pallas as pl
from jax.experimental.pallas import tpu as pltpu
from jax.sharding import PartitionSpec as P

SIDE = 32
CHAN = 3
KSIZE = 5
MAP = SIDE - KSIZE + 1
HALF = MAP // 2
TALL, WIDE = 2, 7
WROWS, WCOLS = TALL + KSIZE - 1, (WIDE + KSIZE - 1) * CHAN
TAPS = KSIZE * KSIZE * CHAN
OUTS = TALL * WIDE
DEPTH = 256
SPAN = 640
WIN = (HALF // TALL) * (HALF // WIDE)
EXT = 80


def window_picks():
    picks = np.zeros((MAP // WIDE, 2, SPAN, DEPTH), ml_dtypes.bfloat16)
    for g in range(MAP // WIDE):
        for par in range(2):
            for row in range(WROWS):
                for t in range(WCOLS):
                    picks[g, par, par * 64 + row * SIDE * CHAN + g * WIDE * CHAN + t, row * WCOLS + t] = 1
    return picks


def tap_picks():
    picks = np.zeros((OUTS, DEPTH, EXT), ml_dtypes.bfloat16)
    for a in range(TALL):
        for b in range(WIDE):
            for d in range(KSIZE):
                for t in range(KSIZE * CHAN):
                    picks[a * WIDE + b, (a + d) * WCOLS + b * CHAN + t, d * KSIZE * CHAN + t] = 1
            for extra in range(3):
                picks[a * WIDE + b, WROWS * WCOLS + extra, TAPS + extra] = 1
    return picks


def order_picks(filt):
    picks = np.zeros((4 * filt, 4 * filt), ml_dtypes.bfloat16)
    for q in range(4):
        for f in range(filt):
            picks[q * filt + f, f * 4 + q] = 1
    return picks


def conv_kernel(x_ref, fb_ref, wp_ref, tp_ref, op_ref, out_ref, left, band, quad):
    count = x_ref.shape[0]
    blocks = out_ref.shape[0]
    filt = out_ref.shape[2] // 4
    half_rows = HALF // TALL

    def make_band(o, carry):
        band[o] = jnp.dot(tp_ref[o], fb_ref[...], preferred_element_type=jnp.float32).astype(jnp.bfloat16)
        return carry

    lax.fori_loop(0, OUTS, make_band, 0)
    lanes = lax.broadcasted_iota(jnp.int32, (1, DEPTH), 1)
    ones = jnp.where((lanes >= WROWS * WCOLS) & (lanes < WROWS * WCOLS + 3), 1.0, 0.0)
    for g in range(MAP // WIDE):
        for par in range(2):
            for k in range(half_rows):
                start = 384 * k + 128 * par
                win = jnp.dot(x_ref[:, start : start + SPAN], wp_ref[g, par], preferred_element_type=jnp.float32)
                i2 = 2 * k + par
                q = (i2 // half_rows) * 2 + g // 2
                slot = (i2 % half_rows) * 2 + g % 2
                left[q, slot * count : (slot + 1) * count, :] = (win + ones).astype(jnp.bfloat16)
    for n in range(blocks // 2):
        for q in range(4):

            def one(o, acc):
                resp = jnp.dot(
                    left[q], band[o, :, n * 2 * filt : (n + 1) * 2 * filt], preferred_element_type=jnp.float32
                )
                resp = jnp.maximum(resp, 0.0)
                return acc + resp.reshape(WIN, count, 2 * filt).sum(axis=0)

            acc = lax.fori_loop(0, OUTS, one, jnp.zeros((count, 2 * filt), jnp.float32))
            acc = (acc / (HALF * HALF)).astype(jnp.bfloat16)
            for h in range(2):
                quad[2 * n + h, :, q * filt : (q + 1) * filt] = acc[:, h * filt : (h + 1) * filt]
    for b in range(blocks):
        out_ref[b] = jnp.dot(quad[b], op_ref[...], preferred_element_type=jnp.float32).astype(jnp.bfloat16)


def conv_feats(images, bank):
    count = images.shape[0]
    filt = 128
    blocks = bank.shape[1] // filt
    vmem = pl.BlockSpec(memory_space=pltpu.VMEM)
    return pl.pallas_call(
        conv_kernel,
        out_shape=jax.ShapeDtypeStruct((blocks, count, 4 * filt), jnp.bfloat16),
        in_specs=[vmem] * 5,
        out_specs=vmem,
        scratch_shapes=[
            pltpu.VMEM((4, WIN * count, DEPTH), jnp.bfloat16),
            pltpu.VMEM((OUTS, DEPTH, blocks * filt), jnp.bfloat16),
            pltpu.VMEM((blocks, count, 4 * filt), jnp.bfloat16),
        ],
        compiler_params=pltpu.CompilerParams(vmem_limit_bytes=48 * 2**20),
    )(images, bank, window_picks(), tap_picks(), order_picks(filt))


def invert_block(rows):
    slabs = len(rows)
    lane = lax.broadcasted_iota(jnp.int32, (8, 128), 1)
    sub = lax.broadcasted_iota(jnp.int32, (8, 128), 0)
    for step in range(slabs * 2):
        k = 4 * step
        t, off = k // 8, k % 8
        own = rows[t]
        r = [jnp.broadcast_to(own[off + i : off + i + 1, :], (8, 128)) for i in range(4)]
        a = [[None] * 4 for _ in range(4)]
        for i in range(4):
            for j in range(i, 4):
                a[i][j] = jnp.broadcast_to(r[i][:, k + j : k + j + 1], (8, 128))
        inv = 1.0 / (a[0][0] * a[1][1] - a[0][1] * a[0][1])
        p00, p01, p11 = a[1][1] * inv, -a[0][1] * inv, a[0][0] * inv
        u00 = p00 * a[0][2] + p01 * a[1][2]
        u01 = p00 * a[0][3] + p01 * a[1][3]
        u10 = p01 * a[0][2] + p11 * a[1][2]
        u11 = p01 * a[0][3] + p11 * a[1][3]
        s00 = a[2][2] - (a[0][2] * u00 + a[1][2] * u10)
        s01 = a[2][3] - (a[0][2] * u01 + a[1][2] * u11)
        s11 = a[3][3] - (a[0][3] * u01 + a[1][3] * u11)
        sinv = 1.0 / (s00 * s11 - s01 * s01)
        q00, q01, q11 = s11 * sinv, -s01 * sinv, s00 * sinv
        v00 = u00 * q00 + u01 * q01
        v01 = u00 * q01 + u01 * q11
        v10 = u10 * q00 + u11 * q01
        v11 = u10 * q01 + u11 * q11
        d = [
            [p00 + v00 * u00 + v01 * u01, p01 + v00 * u10 + v01 * u11, -v00, -v01],
            [None, p11 + v10 * u10 + v11 * u11, -v10, -v11],
            [None, None, q00, q01],
            [None, None, None, q11],
        ]
        for i in range(4):
            for j in range(i):
                d[i][j] = d[j][i]
        inside = (lane >= k) & (lane < k + 4)
        rt = [jnp.where(inside, jnp.where(lane == k + i, 1.0, 0.0), r[i]) for i in range(4)]
        new = [d[i][0] * rt[0] + d[i][1] * rt[1] + d[i][2] * rt[2] + d[i][3] * rt[3] for i in range(4)]
        out = []
        for s in range(slabs):
            c = [jnp.broadcast_to(rows[s][:, k + i : k + i + 1], (8, 128)) for i in range(4)]
            base = jnp.where(inside, 0.0, rows[s])
            val = base - (c[0] * new[0] + c[1] * new[1]) - (c[2] * new[2] + c[3] * new[3])
            if s == t:
                for i in range(4):
                    val = jnp.where(sub == off + i, new[i], val)
            out.append(val)
        rows = out
    return rows


def dot32(a, b, dims=((1,), (0,))):
    return lax.dot_general(a, b, (dims, ((), ())), precision=lax.Precision.HIGHEST, preferred_element_type=jnp.float32)


def solve_kernel(total, gram_ref, cross_ref, out_ref, mat, diag, upper):
    size = gram_ref.shape[0]
    steps = size // 128
    row = lax.broadcasted_iota(jnp.int32, (size, size), 0)
    col = lax.broadcasted_iota(jnp.int32, (size, size), 1)
    mat[...] = gram_ref[...] / total + jnp.where(row == col, 0.5, 0.0)
    out_ref[...] = cross_ref[...] / total
    for k in range(steps):
        lo, hi = 128 * k, 128 * (k + 1)
        rows = invert_block([mat[lo + 8 * s : lo + 8 * s + 8, lo:hi] for s in range(16)])
        inv = jnp.concatenate(rows, axis=0)
        diag[k] = inv
        if hi < size:
            side = mat[lo:hi, hi:]
            ratio = dot32(inv, side)
            upper[lo:hi, hi:] = ratio
            mat[hi:, hi:] = mat[hi:, hi:] - dot32(side, ratio, ((0,), (0,)))
            out_ref[hi:, :] = out_ref[hi:, :] - dot32(ratio, out_ref[lo:hi, :], ((0,), (0,)))
    for k in reversed(range(steps)):
        lo, hi = 128 * k, 128 * (k + 1)
        val = dot32(diag[k], out_ref[lo:hi, :])
        if hi < size:
            val = val - dot32(upper[lo:hi, hi:], out_ref[hi:, :])
        out_ref[lo:hi, :] = val


def ridge_solve(gram, cross, total):
    size = gram.shape[0]
    vmem = pl.BlockSpec(memory_space=pltpu.VMEM)
    return pl.pallas_call(
        functools.partial(solve_kernel, total),
        out_shape=jax.ShapeDtypeStruct(cross.shape, jnp.float32),
        in_specs=[vmem] * 2,
        out_specs=vmem,
        scratch_shapes=[
            pltpu.VMEM((size, size), jnp.float32),
            pltpu.VMEM((size // 128, 128, 128), jnp.float32),
            pltpu.VMEM((size, size), jnp.float32),
        ],
        compiler_params=pltpu.CompilerParams(vmem_limit_bytes=48 * 2**20),
    )(gram, cross)


def split_parts(values):
    upper = lax.reduce_precision(values, 8, 7)
    lower = lax.reduce_precision(values - upper, 8, 7)
    return (upper.astype(jnp.bfloat16), lower.astype(jnp.bfloat16))


def left_product(feats, other):
    return lax.dot_general(feats, other, (((0,), (0,)), ((), ())), preferred_element_type=jnp.float32)


def filter_rows(filters, biases):
    first = lax.reduce_precision(biases, 8, 7)
    second = lax.reduce_precision(biases - first, 8, 7)
    extra = jnp.stack([first, second, biases - first - second]).astype(jnp.bfloat16)
    fill = jnp.zeros((EXT - TAPS - 3, filters.shape[1]), jnp.bfloat16)
    return jnp.concatenate([filters, extra, fill], axis=0)


def shards(images, labels, predictions, filters, biases):
    share = images.shape[0]
    total_images = share * lax.axis_size("feat") * lax.axis_size("dp")
    bank = lax.all_gather(filter_rows(filters, biases), "feat", axis=1, tiled=True)
    own = conv_feats(images, bank)
    feats = lax.all_to_all(own, "feat", split_axis=0, concat_axis=0, tiled=True)
    feats = feats.reshape(feats.shape[0] * share, feats.shape[2])
    residual = (
        labels[:, None] == jnp.arange(predictions.shape[1], dtype=jnp.int32)[None, :]
    ).astype(jnp.float32) - predictions
    res_upper, res_lower = split_parts(residual)
    gram = left_product(feats, feats)
    cross = left_product(feats, res_upper) + left_product(feats, res_lower)
    gram, cross = lax.psum((gram, cross), "dp")
    solved = ridge_solve(gram, cross, total_images)
    sol_upper, sol_lower = split_parts(solved)
    fitted = lax.psum_scatter(
        (
            jnp.dot(feats, sol_upper, preferred_element_type=jnp.float32)
            + jnp.dot(feats, sol_lower, preferred_element_type=jnp.float32)
        ).astype(jnp.bfloat16),
        "feat",
        scatter_dimension=0,
        tiled=True,
    ).astype(jnp.float32)
    mine = lax.dynamic_slice_in_dim(residual, lax.axis_index("feat") * share, share, 0)
    return (solved, mine - fitted)


def solution(mesh):
    placed = (P(("dp", "feat"), None), P("dp"), P("dp", None), P(None, "feat"), P("feat"))
    return jax.shard_map(
        shards,
        mesh=mesh,
        in_specs=placed,
        out_specs=(P("feat", None), P(("dp", "feat"), None)),
        check_vma=False,
    )
```

time: 397 us -> 227 us (0.57); the launches traced: 392 us -> 227 us
  other arithmetic: 159 us -> 2.46 us
  Pallas kernels: 0 us -> 80.6 us
  matrix products: 65.5 us -> 3.95 us
  waiting for transfers between devices: 129 us -> 95.6 us
  blocking collectives: 0 us -> 13.7 us
  local copies, waits for them, and re-layouts: 21.8 us -> 12.5 us
    another operation x18 -> x1, other arithmetic: 119 us -> 0.66 us  [filter_rows(): jnp.stack([first, second, biases - first - second]).astype(jnp.bfloat16)]
    pallas_call x0 -> x2, Pallas kernels: none -> 80.6 us  [the longest x1 41.8 us: conv_feats(): pl.pallas_call(conv_kernel, out_shape=jax.ShapeDtypeStruct((blocks, count...]
    conv_general_dilated x2 -> x0, matrix products: 38.2 us -> none  [conv_pool(): lax.conv_general_dilated(pics, kernel, (1, 1), 'VALID', dimension_numbers...]
    all_gather x1 -> x0, waiting for transfers between devices: 38 us -> none  [shards(): piece = lax.all_gather(images, 'feat', axis=0, tiled=True)]
    reduce_sum x2 -> x0, other arithmetic: 32.3 us -> none  [conv_pool(): response.reshape(count, 2, half, 2, half, filt_count).mean(axis=(2, 4))]
    another operation x20 -> x0, matrix products: 20.8 us -> none  [the longest x7 7.85 us: chol_solve(): lax.linalg.triangular_solve(factor, middle, left_side=True, lower=True, t...]
    all_gather x0 -> x1, blocking collectives: none -> 13.7 us  [shards(): lax.all_gather(filter_rows(filters, biases), 'feat', axis=1, tiled=True)]
    another operation x17 -> x0, local copies, waits for them, and re-layouts: 10.2 us -> none
where the time goes in v1:
time: 227 us
  waiting for transfers between devices  95.6 us (42%)
  Pallas kernels  80.6 us (36%)
  between operations  14.1 us (6%)
  blocking collectives  13.7 us (6%)
  local copies, waits for them, and re-layouts  12.5 us (6%)
  starting transfers between devices  3.96 us (2%)
  matrix products  3.95 us (2%)
  other arithmetic  2.46 us (1%)
    psum x1, waiting for transfers between devices, shards(): gram, cross = lax.psum((gram, cross), 'dp')  69.3 us
    pallas_call x1, Pallas kernels, conv_feats(): pl.pallas_call(conv_kernel, out_shape=jax.ShapeDtypeStruct((blocks, count...  41.8 us
    pallas_call x1, Pallas kernels, ridge_solve(): pl.pallas_call(functools.partial(solve_kernel, total), out_shape=jax.Shap...  38.8 us
    reduce_scatter x1, waiting for transfers between devices, shards(): lax.psum_scatter((jnp.dot(feats, sol_upper, preferred_element_type=jnp.fl...  20 us
    all_gather x1, blocking collectives, shards(): lax.all_gather(filter_rows(filters, biases), 'feat', axis=1, tiled=True)  13.7 us
    unnamed x18, local copies, waits for them, and re-layouts  9.9 us
    all_to_all x1, waiting for transfers between devices, shards(): feats = lax.all_to_all(own, 'feat', split_axis=0, concat_axis=0, tiled=True)  6.25 us
  transfers between devices with their start and end apart: 3, of which 3 were waited for; matrix products, arithmetic and copies ran while one was open for 1% of the time, Pallas kernels for 0%

profile of v1, /device:TPU:0, one launch (start us, length us, event | category | flops | bytes accessed | tf_op | source)
XLA Modules:
  0.0 226.9 jit_solution(9294946321728020967)
XLA Ops:
  7.2 0.7 fusion.12
  7.8 0.8 concatenate.4
  8.6 13.7 %all_gather.3.fb_ref = bf16[80,512]{1,0:T(8,128)(2,1)S(1)} all-gather(bf16[80,128]{1,0:T(8,128)(2,1)S(1)} %concatenate.4), channel_id=1, replica_groups=mesh['dp'=8,'feat'=4] {'feat'}, dimensions={1}, use_global_device_ids=true | all-gather | bytes 102400 | tf_op jit(solution)/shard_map/all_gather | solution.py:237
  22.3 0.0 copy-start
  22.3 1.7 copy-done
  24.1 0.0 copy-start.3
  24.1 1.2 copy-done.3
  25.2 0.0 copy-start.4
  25.2 1.0 copy-done.4
  26.3 0.0 copy-start.5
  26.3 1.0 copy-done.5
  27.3 0.0 copy-start.6
  27.3 41.8 %shard_map.95 = bf16[4,64,512]{2,1,0:T(8,128)(2,1)} custom-call(bf16[64,3072]{1,0:T(8,128)(2,1)S(1)} %copy-done.5, bf16[80,512]{1,0:T(8,128)(2,1)S(1)} %all_gather.3.fb_ref, bf16[4,2,640,256]{3,2,1,0:T(8,128)(2,1)S(1)} %copy-done, bf16[14,256,80]{2,1,0:T(8,128)(2,1)S(1)} %copy-done.3, bf16[512,512]{1,0:T(8,128)(2,1)S(1)} %copy-done.4), custom_call_target="tpu_custom_call" | custom-call | tf_op jit(solution)/shard_map/pallas_call | solution.py:102
  69.0 0.0 copy-start.7
  69.0 3.7 %all-to-all-start = ((bf16[4,64,512]{2,1,0:T(8,128)(2,1)}), bf16[4,64,512]{2,1,0:T(8,128)(2,1)S(1)}, u32[]{:S(2)}, u32[]{:S(2)}) async-start(bf16[4,64,512]{2,1,0:T(8,128)(2,1)} %shard_map.95), calls=%async_computation | async-start | bytes 524288 | tf_op jit(solution)/shard_map/all_to_all | solution.py:239
  72.8 0.0 all-reduce.3.cloned.1.call-start
  72.8 0.0 copy-done.6
  72.8 0.3 copy.14
  73.1 0.0 copy-done.7
  73.1 0.2 convert_subtract_fusion
  73.3 6.2 %all-to-all-done = bf16[4,64,512]{2,1,0:T(8,128)(2,1)S(1)} async-done(((bf16[4,64,512]{2,1,0:T(8,128)(2,1)}), bf16[4,64,512]{2,1,0:T(8,128)(2,1)S(1)}, u32[]{:S(2)}, u32[]{:S(2)}) %all-to-all-start) | async-done | bytes 262176 | tf_op jit(solution)/shard_map/all_to_all | solution.py:239
  79.5 0.5 fusion.8
  80.0 0.5 convolution_add_fusion
  80.5 1.8 copy.15
  82.4 1.3 convolution_bitcast_fusion
  83.7 0.0 all-reduce.3.cloned.1.call-update
  83.7 0.2 reduce-scatter.2.cloned.1.call-start
  83.9 69.3 %all-reduce.3.cloned.1.call-done = (f32[512,512]{1,0:T(8,128)}, f32[512,1000]{1,0:T(8,128)}) async-done(((f32[512,512]{1,0:T(8,128)}, f32[512,1000]{1,0:T(8,128)}), (f32[512,512]{1,0:T(8,128)}, f32[512,1000]{1,0:T(8,128)})) %all-reduce.3.cloned.1.call-update) | async-done | bytes 3096592 | tf_op jit(solution)/shard_map/psum | solution.py:247
  153.3 0.0 copy-start.1
  153.3 1.6 copy-done.1
  154.8 0.0 copy-start.2
  154.8 1.2 copy-done.2
  156.1 38.8 %shard_map.96 = f32[512,1000]{1,0:T(8,128)S(1)} custom-call(f32[512,512]{1,0:T(8,128)S(1)} %copy-done.2, f32[512,1000]{1,0:T(8,128)S(1)} %copy-done.1), custom_call_target="tpu_custom_call" | custom-call | tf_op jit(solution)/shard_map/pallas_call | solution.py:202
  194.9 0.4 fusion.6
  195.3 1.3 fusion.2
  196.6 0.0 reduce-scatter.2.cloned.1.call-update
  196.6 1.8 copy.16
  198.4 20.0 %reduce-scatter.2.cloned.1.call-done = bf16[64,1000]{1,0:T(8,128)(2,1)} async-done(((bf16[256,1000]{1,0:T(8,128)(2,1)}), bf16[64,1000]{1,0:T(8,128)(2,1)}) %reduce-scatter.2.cloned.1.call-update) | async-done | bytes 128016 | tf_op jit(solution)/shard_map/reduce_scatter | solution.py:250
  218.4 1.6 convert_subtract_fusion.1
  (1 shorter events, 0.0 us)
Async XLA Ops:
  22.3 1.7 copy-start
  24.1 1.2 copy-start.3
  25.2 1.0 copy-start.4
  26.3 1.0 copy-start.5
  27.3 45.5 %copy-start.6 = (f32[256,1000]{0,1:T(8,128)S(1)}, f32[256,1000]{0,1:T(8,128)}, u32[]{:S(2)}) copy-start(f32[256,1000]{0,1:T(8,128)} %param.10) | copy-start | bytes 3072004
  69.0 4.1 %copy-start.7 = (s32[256]{0:T(256)S(1)}, s32[256]{0:T(256)}, u32[]{:S(2)}) copy-start(s32[256]{0:T(256)} %param.9) | copy-start | bytes 3076
  69.0 10.5 %all-to-all-start = ((bf16[4,64,512]{2,1,0:T(8,128)(2,1)}), bf16[4,64,512]{2,1,0:T(8,128)(2,1)S(1)}, u32[]{:S(2)}, u32[]{:S(2)}) async-start(bf16[4,64,512]{2,1,0:T(8,128)(2,1)} %shard_map.95), calls=%async_computation | async-start | bytes 524288 | tf_op jit(solution)/shard_map/all_to_all | solution.py:239
  72.8 80.5 %all-reduce.3.cloned.1.call-start = ((), (), s32[]{:S(2)}) async-start(), calls=%async_computation.3 | async-start | bytes 6291456 | tf_op jit(solution)/shard_map/psum | solution.py:247
  83.7 134.8 %reduce-scatter.2.cloned.1.call-start = ((), (), s32[]{:S(2)}) async-start(), calls=%async_computation.2 | async-start | bytes 655360 | tf_op jit(solution)/shard_map/reduce_scatter | solution.py:250
  153.3 1.6 copy-start.1
  154.8 1.2 copy-start.2
Sparse Core Ops, SparseCore 0:
  83.8 69.4 all-reduce.2
  196.7 21.6 reduce-scatter.1

commit v2 on v1

--- a/solution.py
+++ b/solution.py
@@ -79,14 +79,17 @@
     for n in range(blocks // 2):
         for q in range(4):
 
-            def one(o, acc):
-                resp = jnp.dot(
-                    left[q], band[o, :, n * 2 * filt : (n + 1) * 2 * filt], preferred_element_type=jnp.float32
-                )
-                resp = jnp.maximum(resp, 0.0)
-                return acc + resp.reshape(WIN, count, 2 * filt).sum(axis=0)
-
-            acc = lax.fori_loop(0, OUTS, one, jnp.zeros((count, 2 * filt), jnp.float32))
+            def some(step, acc):
+                for part in range(TALL):
+                    o = step * TALL + part
+                    resp = jnp.dot(
+                        left[q], band[o, :, n * 2 * filt : (n + 1) * 2 * filt], preferred_element_type=jnp.float32
+                    )
+                    resp = jnp.maximum(resp, 0.0)
+                    acc = acc + resp.reshape(WIN, count, 2 * filt).sum(axis=0)
+                return acc
+
+            acc = lax.fori_loop(0, WIDE, some, jnp.zeros((count, 2 * filt), jnp.float32))
             acc = (acc / (HALF * HALF)).astype(jnp.bfloat16)
             for h in range(2):
                 quad[2 * n + h, :, q * filt : (q + 1) * filt] = acc[:, h * filt : (h + 1) * filt]
@@ -170,12 +173,15 @@
     return lax.dot_general(a, b, (dims, ((), ())), precision=lax.Precision.HIGHEST, preferred_element_type=jnp.float32)
 
 
-def solve_kernel(total, gram_ref, cross_ref, out_ref, mat, diag, upper):
-    size = gram_ref.shape[0]
+def solve_kernel(total, top_ref, corner_ref, cross_ref, out_ref, mat, diag, upper):
+    size = cross_ref.shape[0]
+    half = size // 2
     steps = size // 128
     row = lax.broadcasted_iota(jnp.int32, (size, size), 0)
     col = lax.broadcasted_iota(jnp.int32, (size, size), 1)
-    mat[...] = gram_ref[...] / total + jnp.where(row == col, 0.5, 0.0)
+    mat[...] = jnp.where(row == col, 0.5, 0.0)
+    mat[:half, :] = mat[:half, :] + top_ref[...] / total
+    mat[half:, half:] = mat[half:, half:] + corner_ref[...] / total
     out_ref[...] = cross_ref[...] / total
     for k in range(steps):
         lo, hi = 128 * k, 128 * (k + 1)
@@ -196,13 +202,13 @@
         out_ref[lo:hi, :] = val
 
 
-def ridge_solve(gram, cross, total):
-    size = gram.shape[0]
+def ridge_solve(top, corner, cross, total):
+    size = cross.shape[0]
     vmem = pl.BlockSpec(memory_space=pltpu.VMEM)
     return pl.pallas_call(
         functools.partial(solve_kernel, total),
         out_shape=jax.ShapeDtypeStruct(cross.shape, jnp.float32),
-        in_specs=[vmem] * 2,
+        in_specs=[vmem] * 3,
         out_specs=vmem,
         scratch_shapes=[
             pltpu.VMEM((size, size), jnp.float32),
@@ -210,7 +216,7 @@
             pltpu.VMEM((size, size), jnp.float32),
         ],
         compiler_params=pltpu.CompilerParams(vmem_limit_bytes=48 * 2**20),
-    )(gram, cross)
+    )(top, corner, cross)
 
 
 def split_parts(values):
@@ -242,20 +248,21 @@
         labels[:, None] == jnp.arange(predictions.shape[1], dtype=jnp.int32)[None, :]
     ).astype(jnp.float32) - predictions
     res_upper, res_lower = split_parts(residual)
-    gram = left_product(feats, feats)
+    half = feats.shape[1] // 2
+    top = left_product(feats[:, :half], feats)
+    corner = left_product(feats[:, half:], feats[:, half:])
     cross = left_product(feats, res_upper) + left_product(feats, res_lower)
-    gram, cross = lax.psum((gram, cross), "dp")
-    solved = ridge_solve(gram, cross, total_images)
+    top, corner, cross = lax.psum((top, corner, cross), "dp")
+    solved = ridge_solve(top, corner, cross, total_images)
     sol_upper, sol_lower = split_parts(solved)
-    fitted = lax.psum_scatter(
+    fitted = (
         (
             jnp.dot(feats, sol_upper, preferred_element_type=jnp.float32)
             + jnp.dot(feats, sol_lower, preferred_element_type=jnp.float32)
-        ).astype(jnp.bfloat16),
-        "feat",
-        scatter_dimension=0,
-        tiled=True,
-    ).astype(jnp.float32)
+        ).astype(jnp.bfloat16)
+    )
+    parts = lax.all_to_all(fitted, "feat", split_axis=0, concat_axis=0, tiled=True)
+    fitted = parts.reshape(-1, share, parts.shape[1]).astype(jnp.float32).sum(axis=0)
     mine = lax.dynamic_slice_in_dim(residual, lax.axis_index("feat") * share, share, 0)
     return (solved, mine - fitted)
 

time: 227 us -> 214 us (0.943)
  Pallas kernels: 80.6 us -> 68.5 us
  waiting for transfers between devices: 95.6 us -> 86 us
  starting transfers between devices: 3.96 us -> 8.32 us
  local copies, waits for them, and re-layouts: 12.5 us -> 15.3 us
    reduce_scatter x1 -> x0, waiting for transfers between devices: 20 us -> none  [shards(): lax.psum_scatter((jnp.dot(feats, sol_upper, preferred_element_type=jnp.fl...]
    all_to_all x0 -> x1, waiting for transfers between devices: none -> 12.5 us  [shards(): lax.all_to_all(fitted, 'feat', split_axis=0, concat_axis=0, tiled=True)]
    pallas_call x1, Pallas kernels: 41.8 us -> 29.8 us  [conv_feats(): pl.pallas_call(conv_kernel, out_shape=jax.ShapeDtypeStruct((blocks, count...]
    all_to_all x0 -> x1, starting transfers between devices: none -> 4.59 us  [shards(): lax.all_to_all(fitted, 'feat', split_axis=0, concat_axis=0, tiled=True)]
    unnamed x18 -> x20, local copies, waits for them, and re-layouts: 9.9 us -> 10.7 us
where the time goes in v2:
time: 214 us
  waiting for transfers between devices  86 us (40%)
  Pallas kernels  68.5 us (32%)
  local copies, waits for them, and re-layouts  15.3 us (7%)
  between operations  14.1 us (7%)
  blocking collectives  13.7 us (6%)
  starting transfers between devices  8.32 us (4%)
  matrix products  4.8 us (2%)
  other arithmetic  2.73 us (1%)
    psum x1, waiting for transfers between devices, shards(): top, corner, cross = lax.psum((top, corner, cross), 'dp')  67.3 us
    pallas_call x1, Pallas kernels, ridge_solve(): pl.pallas_call(functools.partial(solve_kernel, total), out_shape=jax.Shap...  38.8 us
    pallas_call x1, Pallas kernels, conv_feats(): pl.pallas_call(conv_kernel, out_shape=jax.ShapeDtypeStruct((blocks, count...  29.8 us
    all_gather x1, blocking collectives, shards(): lax.all_gather(filter_rows(filters, biases), 'feat', axis=1, tiled=True)  13.7 us
    all_to_all x1, waiting for transfers between devices, shards(): lax.all_to_all(fitted, 'feat', split_axis=0, concat_axis=0, tiled=True)  12.5 us
    unnamed x20, local copies, waits for them, and re-layouts  10.7 us
    all_to_all x1, waiting for transfers between devices, shards(): feats = lax.all_to_all(own, 'feat', split_axis=0, concat_axis=0, tiled=True)  6.25 us
    all_to_all x1, starting transfers between devices, shards(): lax.all_to_all(fitted, 'feat', split_axis=0, concat_axis=0, tiled=True)  4.59 us
  transfers between devices with their start and end apart: 3, of which 3 were waited for; matrix products, arithmetic and copies ran while one was open for 1% of the time, Pallas kernels for 0%

profile of v2, /device:TPU:0, one launch (start us, length us, event | category | flops | bytes accessed | tf_op | source)
XLA Modules:
  0.0 213.5 jit_solution(3826168152862575730)
XLA Ops:
  7.2 0.7 fusion.16
  7.8 0.8 concatenate.4
  8.6 13.7 %all_gather.3.fb_ref = bf16[80,512]{1,0:T(8,128)(2,1)S(1)} all-gather(bf16[80,128]{1,0:T(8,128)(2,1)S(1)} %concatenate.4), channel_id=1, replica_groups=mesh['dp'=8,'feat'=4] {'feat'}, dimensions={1}, use_global_device_ids=true | all-gather | bytes 102400 | tf_op jit(solution)/shard_map/all_gather | solution.py:243
  22.3 0.0 copy-start
  22.3 1.7 copy-done
  24.1 0.0 copy-start.2
  24.1 1.2 copy-done.2
  25.2 0.0 copy-start.3
  25.2 1.0 copy-done.3
  26.3 0.0 copy-start.5
  26.3 1.0 copy-done.5
  27.3 0.0 copy-start.7
  27.3 29.8 %shard_map.95 = bf16[4,64,512]{2,1,0:T(8,128)(2,1)} custom-call(bf16[64,3072]{1,0:T(8,128)(2,1)S(1)} %copy-done.5, bf16[80,512]{1,0:T(8,128)(2,1)S(1)} %all_gather.3.fb_ref, bf16[4,2,640,256]{3,2,1,0:T(8,128)(2,1)S(1)} %copy-done, bf16[14,256,80]{2,1,0:T(8,128)(2,1)S(1)} %copy-done.2, bf16[512,512]{1,0:T(8,128)(2,1)S(1)} %copy-done.3), custom_call_target="tpu_custom_call" | custom-call | tf_op jit(solution)/shard_map/pallas_call | solution.py:105
  57.0 0.0 copy-start.8
  57.0 3.7 %all-to-all-start = ((bf16[4,64,512]{2,1,0:T(8,128)(2,1)}), bf16[4,64,512]{2,1,0:T(8,128)(2,1)S(1)}, u32[]{:S(2)}, u32[]{:S(2)}) async-start(bf16[4,64,512]{2,1,0:T(8,128)(2,1)} %shard_map.95), calls=%async_computation | async-start | bytes 524288 | tf_op jit(solution)/shard_map/all_to_all | solution.py:245
  60.8 0.0 all-reduce.3.cloned.1.call-start
  60.8 0.0 copy-done.7
  60.8 0.3 copy.19
  61.1 0.0 copy-done.8
  61.1 0.2 convert_subtract_fusion
  61.3 6.2 %all-to-all-done = bf16[4,64,512]{2,1,0:T(8,128)(2,1)S(1)} async-done(((bf16[4,64,512]{2,1,0:T(8,128)(2,1)}), bf16[4,64,512]{2,1,0:T(8,128)(2,1)S(1)}, u32[]{:S(2)}, u32[]{:S(2)}) %all-to-all-start) | async-done | bytes 262176 | tf_op jit(solution)/shard_map/all_to_all | solution.py:245
  67.5 1.0 fusion.11
  68.6 0.9 fusion.9
  69.5 0.5 fusion.8
  70.0 0.5 convolution_add_fusion
  70.5 1.8 copy.20
  72.3 0.0 all-reduce.3.cloned.1.call-update
  72.4 67.3 %all-reduce.3.cloned.1.call-done = (f32[256,512]{1,0:T(8,128)}, f32[256,256]{1,0:T(8,128)}, f32[512,1000]{1,0:T(8,128)}) async-done(((f32[256,512]{1,0:T(8,128)}, f32[256,256]{1,0:T(8,128)}, f32[512,1000]{1,0:T(8,128)}), (f32[256,512]{1,0:T(8,128)}, f32[256,256]{1,0:T(8,128)}, f32[512,1000]{1,0:T(8,128)})) %all-reduce.3.cloned.1.call-update) | async-done | bytes 2834448 | tf_op jit(solution)/shard_map/psum | solution.py:255
  139.7 0.0 copy-start.1
  139.7 1.6 copy-done.1
  141.3 0.0 copy-start.4
  141.3 1.0 copy-done.4
  142.3 0.0 copy-start.6
  142.3 0.9 copy-done.6
  143.2 38.8 %shard_map.96 = f32[512,1000]{1,0:T(8,128)S(1)} custom-call(f32[256,512]{1,0:T(8,128)S(1)} %copy-done.4, f32[256,256]{1,0:T(8,128)S(1)} %copy-done.6, f32[512,1000]{1,0:T(8,128)S(1)} %copy-done.1), custom_call_target="tpu_custom_call" | custom-call | tf_op jit(solution)/shard_map/pallas_call | solution.py:208
  182.0 0.5 fusion.6
  182.6 1.3 fusion.2
  183.9 2.0 copy.21
  186.0 4.6 %all-to-all-start.1 = ((bf16[4,64,1000]{2,1,0:T(8,128)(2,1)}), bf16[4,64,1000]{2,1,0:T(8,128)(2,1)}, u32[]{:S(2)}, u32[]{:S(2)}) async-start(bf16[4,64,1000]{2,1,0:T(8,128)(2,1)} %bitcast.19), calls=%async_computation.1 | async-start | bytes 1048576 | tf_op jit(solution)/shard_map/all_to_all | solution.py:264
  190.5 1.8 copy.22
  192.3 12.5 %all-to-all-done.1 = bf16[4,64,1000]{2,1,0:T(8,128)(2,1)} async-done(((bf16[4,64,1000]{2,1,0:T(8,128)(2,1)}), bf16[4,64,1000]{2,1,0:T(8,128)(2,1)}, u32[]{:S(2)}, u32[]{:S(2)}) %all-to-all-start.1) | async-done | bytes 512032 | tf_op jit(solution)/shard_map/all_to_all | solution.py:264
  204.8 1.1 convert_reduce_fusion
  205.9 0.8 dynamic-slice_subtract_fusion
  (1 shorter events, 0.0 us)
Async XLA Ops:
  22.3 1.7 copy-start
  24.1 1.2 copy-start.2
  25.2 1.0 copy-start.3
  26.3 1.0 copy-start.5
  27.3 33.5 %copy-start.7 = (f32[256,1000]{0,1:T(8,128)S(1)}, f32[256,1000]{0,1:T(8,128)}, u32[]{:S(2)}) copy-start(f32[256,1000]{0,1:T(8,128)} %param.10) | copy-start | bytes 3072004
  57.0 4.1 %copy-start.8 = (s32[256]{0:T(256)S(1)}, s32[256]{0:T(256)}, u32[]{:S(2)}) copy-start(s32[256]{0:T(256)} %param.9) | copy-start | bytes 3076
  57.0 10.5 %all-to-all-start = ((bf16[4,64,512]{2,1,0:T(8,128)(2,1)}), bf16[4,64,512]{2,1,0:T(8,128)(2,1)S(1)}, u32[]{:S(2)}, u32[]{:S(2)}) async-start(bf16[4,64,512]{2,1,0:T(8,128)(2,1)} %shard_map.95), calls=%async_computation | async-start | bytes 524288 | tf_op jit(solution)/shard_map/all_to_all | solution.py:245
  60.8 78.9 %all-reduce.3.cloned.1.call-start = ((), (), s32[]{:S(2)}) async-start(), calls=%async_computation.2 | async-start | bytes 5767168 | tf_op jit(solution)/shard_map/psum | solution.py:255
  139.7 1.6 copy-start.1
  141.3 1.0 copy-start.4
  142.3 0.9 copy-start.6
  186.0 18.8 %all-to-all-start.1 = ((bf16[4,64,1000]{2,1,0:T(8,128)(2,1)}), bf16[4,64,1000]{2,1,0:T(8,128)(2,1)}, u32[]{:S(2)}, u32[]{:S(2)}) async-start(bf16[4,64,1000]{2,1,0:T(8,128)(2,1)} %bitcast.19), calls=%async_computation.1 | async-start | bytes 1048576 | tf_op jit(solution)/shard_map/all_to_all | solution.py:264
Sparse Core Ops, SparseCore 0:
  72.5 67.1 all-reduce.2
